TPU v7x, 32 devices: a whole 2x2x4 slice. The times are simulated.
32 devices in a mesh: freq: 8 (over y, x, core), blk: 4 (over z).
Axes of the slice: x: 2, y: 2, z: 4, core: 2. Of those that a mesh axis runs over, the one named last changes fastest.
Arguments:
- voltages: bfloat16 [1024, 64, 2048], P('freq', 'blk'), may hold values from -6 to 6
- channel_order: int32 [512], replicated, may hold values from 0 to 511, each once
- owner_count: int32 [4], replicated, may hold values from 1 to 192, 512 in all
- channel_good: int32 [512], replicated, may hold values 0 or 1
Outputs:
- visibility: bfloat16 [2, 768, 1024, 640], P(None, 'blk', 'freq')
Inputs may be any that keep to these rules, and one draw needn't show every extreme that they name: `channel_order`: every channel appears once. `owner_count`: the counts sum to 512; the largest is exactly 192.
All inputs are finite; a program needn't handle non-finite values.
Results may differ from a plain program's by a relative error of at most 0.0074.
Values may be sent and summed in bfloat16 or wider, within the bound.
A program may use at most 320 MiB of HBM per device.

v0:
```python
import functools

import jax
import jax.numpy as jnp
import ml_dtypes
import numpy as np
from jax import lax
from jax.experimental import pallas as pl
from jax.experimental.pallas import tpu as pltpu
from jax.sharding import PartitionSpec as P

NSAMP = 2048
NCH = 512
TAPS = 4
CH0 = 256
MESH = pl.DeviceIdType.MESH


def shifted(value, axis, steps):
    count = lax.axis_size(axis)
    first, last = (max(0, -steps), min(count, count - steps))
    return lax.ppermute(value, axis, [(source, source + steps) for source in range(first, last)])


def pfb_window():
    offsets_u = np.arange(TAPS * NSAMP, dtype=np.float64)
    centered = (offsets_u - TAPS * NSAMP / 2) / NSAMP
    hann_taper = 0.5 - 0.5 * np.cos(2 * np.pi * offsets_u / (TAPS * NSAMP))
    window = (np.sinc(centered) * hann_taper).astype(np.float32).reshape(TAPS, NSAMP)
    normalizer = np.float32(1.0 / np.sqrt(np.sum(window.astype(np.float64) ** 2)))
    return (window, normalizer)


def transform_table():
    sample = np.arange(NSAMP, dtype=np.int64)
    channel_id = CH0 + np.arange(NCH, dtype=np.int64)
    angles = 2 * np.pi / NSAMP * (sample[None, :] * channel_id[:, None] % NSAMP)
    return np.stack([np.cos(angles), -np.sin(angles)], axis=0).astype(ml_dtypes.bfloat16)


def slot_tables(channel_order, owner_count, channel_good, capacity):
    starts = jnp.cumsum(owner_count) - owner_count
    positions = jnp.arange(capacity, dtype=jnp.int32)
    filled = positions[None, :] < owner_count[:, None]
    picked = jnp.minimum(starts[:, None] + positions[None, :], NCH - 1)
    channel = jnp.where(filled, channel_order[picked], 0).reshape(-1)
    slot_live = jnp.where(filled.reshape(-1), channel_good[channel], 0)
    return (channel, slot_live)


def exchange_kernel(cycle, owners, chunks, offsets, out_ref, buf_ref, local_sem, z_send, z_recv, f_send, f_recv):
    step_rows = out_ref.shape[1] // chunks
    me_f, me_z = lax.axis_index("freq"), lax.axis_index("blk")
    core = lax.rem(me_f, 2)
    side = lax.rem(me_f // 2, 2)
    mate_core = me_f + 1 - 2 * core
    mate_chip = me_f + 2 - 4 * side
    fours = [o for o in range(4, offsets, 4)]
    twos = [o for o in range(2, offsets, 4)]
    odds = [o for o in range(1, offsets, 2)]

    barrier = pltpu.get_barrier_semaphore()
    greeted = []
    for delta in range(1, owners):
        greeted.append((me_f, lax.rem(me_z + delta, owners)))
    far = sorted({o % cycle for o in fours} | {(cycle - o) % cycle for o in fours})
    for step in far:
        greeted.append((lax.rem(me_f + step, cycle), me_z))
    greeted.append((mate_core, me_z))
    greeted.append((mate_chip, me_z))
    for place in greeted:
        pl.semaphore_signal(barrier, inc=1, device_id=place, device_id_type=MESH)
    pl.semaphore_wait(barrier, len(greeted))

    def rows(c):
        return pl.ds(c * step_rows, step_rows)

    def own_copy(c):
        return pltpu.make_async_copy(
            out_ref.at[me_z, rows(c)], buf_ref.at[0, rows(c), me_z], local_sem.at[c]
        )

    def z_copy(c, delta):
        there = lax.rem(me_z + delta, owners)
        return pltpu.make_async_remote_copy(
            src_ref=out_ref.at[there, rows(c)],
            dst_ref=buf_ref.at[0, rows(c), me_z],
            send_sem=z_send.at[c, delta],
            recv_sem=z_recv.at[c, delta],
            device_id=(me_f, there),
            device_id_type=MESH,
        )

    def f_copy(c, o):
        if o % 4 == 0:
            held, there = 0, lax.rem(me_f + cycle - o, cycle)
        elif o % 4 == 2:
            held, there = o + 2 - 4 * side, mate_chip
        else:
            held, there = o + 1 - 2 * core, mate_core
        return pltpu.make_async_remote_copy(
            src_ref=buf_ref.at[held, rows(c)],
            dst_ref=buf_ref.at[o, rows(c)],
            send_sem=f_send.at[c, o],
            recv_sem=f_recv.at[c, o],
            device_id=(there, me_z),
            device_id_type=MESH,
        )

    @pl.loop(0, chunks)
    def _(c):
        own_copy(c).start()
        for delta in range(1, owners):
            z_copy(c, delta).start()

    @pl.loop(0, chunks + 2)
    def _(step):
        @pl.when(step < chunks)
        def _():
            own_copy(step).wait()
            for delta in range(1, owners):
                z_copy(step, delta).wait_recv()
            for o in fours:
                f_copy(step, o).start()

        @pl.when(jnp.logical_and(step >= 1, step < chunks + 1))
        def _():
            for o in fours:
                f_copy(step - 1, o).wait_recv()
            for o in twos:
                f_copy(step - 1, o).start()

        @pl.when(step >= 2)
        def _():
            for o in twos:
                f_copy(step - 2, o).wait_recv()
            for o in odds:
                f_copy(step - 2, o).start()

    @pl.loop(0, chunks)
    def _(c):
        for delta in range(1, owners):
            z_copy(c, delta).wait_send()
        for o in fours + twos:
            f_copy(c, o).wait_send()
        for o in odds:
            f_copy(c, o).wait()


def exchange(outgoing, cycle, owners, offsets, chunks):
    _, capacity, tile, width = outgoing.shape
    moved = outgoing.size * 2 * (1 + offsets)
    return pl.pallas_call(
        functools.partial(exchange_kernel, cycle, owners, chunks, offsets),
        out_shape=jax.ShapeDtypeStruct((offsets, capacity, owners, tile, width), outgoing.dtype),
        in_specs=[pl.BlockSpec(memory_space=pl.ANY)],
        out_specs=pl.BlockSpec(memory_space=pl.ANY),
        scratch_shapes=[
            pltpu.SemaphoreType.DMA((chunks,)),
            pltpu.SemaphoreType.DMA((chunks, owners)),
            pltpu.SemaphoreType.DMA((chunks, owners)),
            pltpu.SemaphoreType.DMA((chunks, offsets)),
            pltpu.SemaphoreType.DMA((chunks, offsets)),
        ],
        compiler_params=pltpu.CompilerParams(
            collective_id=0, has_side_effects=True, vmem_limit_bytes=16 * 1024 * 1024
        ),
        cost_estimate=pl.CostEstimate(flops=0, bytes_accessed=moved, transcendentals=0),
        name="exchange",
    )(outgoing)


def correlate_kernel(owners, factor_ref, spectra_ref, out_ref):
    offsets, slots, depth, width = spectra_ref.shape
    half = depth // (2 * owners)
    first = pl.program_id(0) * slots
    for m in range(slots):
        scale = factor_ref[first + m]
        own = spectra_ref[0, m]
        swapped = []
        for source in range(owners):
            low = source * 2 * half
            swapped.append(own[low + half : low + 2 * half])
            swapped.append(-own[low : low + half])
        turned = jnp.concatenate(swapped, axis=0)
        left = jnp.concatenate([own.T, turned.T], axis=0)
        for o in range(offsets):
            summed = jnp.dot(left, spectra_ref[o, m], preferred_element_type=jnp.float32) * scale
            summed = summed.astype(jnp.bfloat16)
            out_ref[0, m, :, o * width : (o + 1) * width] = summed[:width]
            out_ref[1, m, :, o * width : (o + 1) * width] = summed[width:]


def correlate(spectra, factor, owners, slots):
    offsets, capacity, depth, width = spectra.shape
    return pl.pallas_call(
        functools.partial(correlate_kernel, owners),
        grid=(capacity // slots,),
        out_shape=jax.ShapeDtypeStruct((2, capacity, width, offsets * width), jnp.bfloat16),
        in_specs=[
            pl.BlockSpec(memory_space=pltpu.SMEM),
            pl.BlockSpec((offsets, slots, depth, width), lambda g: (0, g, 0, 0)),
        ],
        out_specs=pl.BlockSpec((2, slots, width, offsets * width), lambda g: (0, g, 0, 0)),
        compiler_params=pltpu.CompilerParams(vmem_limit_bytes=48 * 1024 * 1024),
        cost_estimate=pl.CostEstimate(
            flops=4 * capacity * depth * width * width * offsets,
            bytes_accessed=2 * spectra.size + 4 * capacity * width * width * offsets,
            transcendentals=0,
        ),
        name="correlate",
    )(factor, spectra)


def body(voltages, channel_order, owner_count, channel_good):
    block_width, frame_count, sample_count = voltages.shape
    cycle_size = lax.axis_size("freq")
    owners = lax.axis_size("blk")
    capacity = 3 * NCH // (2 * owners)
    offset_count = cycle_size // 2 + 1
    frames_all = frame_count * owners
    window, normalizer = pfb_window()
    history = shifted(voltages[:, frame_count - (TAPS - 1) :, :], "blk", 1)
    padded = jnp.concatenate([history, voltages], axis=1)
    filtered = jnp.zeros((block_width, frame_count, sample_count), jnp.float32)
    for k in range(TAPS):
        filtered = filtered + window[k] * padded[:, k : k + frame_count].astype(jnp.float32)
    filtered = filtered.astype(jnp.bfloat16)
    spectra = jnp.einsum(
        "pcs,ifs->cpfi", transform_table(), filtered, preferred_element_type=jnp.float32
    )
    spectra = (spectra * normalizer).astype(jnp.bfloat16)
    channel, slot_live = slot_tables(channel_order, owner_count, channel_good, capacity)
    outgoing = jnp.take(spectra, channel, axis=0, mode="clip").reshape(
        owners, capacity, 2 * frame_count, block_width
    )
    chunks = max(1, capacity // 16)
    arrived = exchange(outgoing, cycle_size, owners, offset_count, chunks)
    arrived = arrived.reshape(offset_count, capacity, owners * 2 * frame_count, block_width)
    factor = (
        lax.dynamic_slice_in_dim(slot_live, lax.axis_index("blk") * capacity, capacity).astype(
            jnp.float32
        )
        / frames_all
    )
    return correlate(arrived, factor, owners, 8)


def solution(mesh):
    in_specs = (P("freq", "blk", None), P(), P(), P())
    out_specs = P(None, "blk", "freq", None)
    return jax.shard_map(body, mesh=mesh, in_specs=in_specs, out_specs=out_specs, check_vma=False)
```

profile of v0, /device:TPU:9, one launch (start us, length us, event | category | flops | bytes accessed | tf_op | source)
XLA Modules:
  0.0 356.4 jit_solution(13670125383860056223)
XLA Ops:
  0.0 3.5 slice.12
  3.5 0.0 copy-start.5
  3.5 0.0 copy-start.6
  3.5 0.0 copy-start.7
  3.5 0.0 copy-start.8
  3.5 1.1 copy.21
  4.7 3.2 collective-permute-start
  7.9 0.8 reduce-window.9
  8.7 0.7 bitcast_subtract_fusion
  9.4 0.1 compare_select_fusion.1
  9.5 0.1 reshape.150
  9.6 5.0 %gather_fusion = s32[768]{0:T(1024)S(1)} fusion(s32[512]{0:T(512)S(1)} %copy-done, s32[1024]{0:T(1024)S(1)} %pad_clamp_fusion.2), kind=kCustom, calls=%fused_computation | custom fusion | bytes 9216 | tf_op jit(solution)/shard_map/gather | solution.py:46
  14.6 0.1 reshape.149
  14.7 0.0 copy-done.9
  14.7 0.1 broadcast_select_fusion.1
  14.7 0.1 select_n.48
  14.8 0.1 reshape.166
  14.9 0.1 iota_compare_fusion
  15.0 0.1 lt.68
  15.1 5.0 %gather_fusion.1 = s32[768]{0:T(1024)S(1)} fusion(s32[512]{0:T(512)S(1)} %copy-done.4, s32[1024]{0:T(1024)S(1)} %pad_clamp_fusion.1), kind=kCustom, calls=%fused_computation.1 | custom fusion | bytes 9216 | tf_op jit(solution)/shard_map/gather | solution.py:47
  20.1 0.1 convert_multiply_fusion.factor_ref
  20.2 21.6 %collective-permute-done = bf16[128,3,2048]{2,0,1:T(8,128)(2,1)S(1)} collective-permute-done((bf16[128,3,2048]{2,0,1:T(8,128)(2,1)S(1)}, bf16[128,3,2048]{2,0,1:T(8,128)(2,1)S(1)}, u32[]{:S(2)}, u32[]{:S(2)}) %collective-permute-start) | collective-permute-done | bytes 1572896 | tf_op jit(solution)/shard_map/ppermute | solution.py:22
  41.9 1.4 copy.15
  43.2 0.0 copy-start.10
  43.3 18.4 %fusion.4 = bf16[128,16,2048,1]{2,1,0,3:T(8,128)(2,1)S(1)} fusion(bf16[128,16,2048]{2,1,0:T(8,128)(2,1)} %param.9, f32[2048]{0:T(1024)S(1)} %copy-done.5, bf16[128,3,2048]{2,1,0:T(4,128)(2,1)S(1)} %copy.15, f32[2048]{0:T(1024)S(1)} %copy-done.6, f32[2048]{0:T(1024)S(1)} %copy-done.7, f32[2048]{0:T(1024)S(1)} %copy-done.8), kind=kLoop, calls=%fused_computation.14 | loop fusion | flops 88080384 | bytes 18382848 | tf_op jit(solution)/shard_map/convert_element_type | solution.py:228
  61.6 24.0 %fusion.5 = bf16[512,2,16,128]{0,3,1,2:T(8,128)(2,1)} fusion(bf16[2,512,2048,1]{2,1,0,3:T(8,128)(2,1)S(1)} %copy-done.10, bf16[128,16,2048,1]{2,1,0,3:T(8,128)(2,1)S(1)} %fusion.4), kind=kOutput, calls=%fused_computation.15 | convolution fusion | flops 8594128896 | bytes 16777216 | tf_op jit(solution)/shard_map/pcs,ifs->cpfi/dot_general | solution.py:229
  85.7 8.0 %copy.17 = bf16[512,2,16,128]{3,2,1,0:T(8,128)(2,1)} copy(bf16[512,2,16,128]{0,3,1,2:T(8,128)(2,1)} %fusion.5) | data formatting | bytes 8388608 | tf_op jit(solution)/shard_map/convert_element_type | solution.py:232
  93.7 7.2 %gather_fusion.2 = bf16[768,2,16,128]{3,2,1,0:T(8,128)(2,1)} fusion(bf16[512,2,16,128]{3,2,1,0:T(8,128)(2,1)} %copy.17, s32[1024]{0:T(1024)S(1)} %pad_clamp_fusion), kind=kCustom, calls=%fused_computation.2 | custom fusion | bytes 12585984 | tf_op jit(solution)/shard_map/jit(_take)/gather | solution.py:234
  100.9 2.8 copy-done.3
  103.7 201.4 %exchange.1 = bf16[5,192,4,32,128]{4,3,2,1,0:T(8,128)(2,1)S(1)} custom-call(bf16[4,192,32,128]{3,2,1,0:T(8,128)(2,1)S(1)} %bitcast.14), custom_call_target="tpu_custom_call" | custom-call | bytes 37748736 | tf_op jit(solution)/shard_map/exchange/pallas_call | solution.py:153
  305.1 10.4 %copy-done.2 = bf16[5,192,4,32,128]{4,3,2,1,0:T(8,128)(2,1)} copy-done((bf16[5,192,4,32,128]{4,3,2,1,0:T(8,128)(2,1)}, bf16[5,192,4,32,128]{4,3,2,1,0:T(8,128)(2,1)S(1)}, u32[]{:S(2)}) %copy-start.2) | copy-done | bytes 31457304
  315.5 40.9 %correlate.1 = bf16[2,192,128,640]{3,2,1,0:T(8,128)(2,1)} custom-call(f32[192]{0:T(256)S(1)} %convert_multiply_fusion.factor_ref, bf16[5,192,128,128]{3,2,1,0:T(8,128)(2,1)} %bitcast.13), custom_call_target="tpu_custom_call" | custom-call | flops 8053063680 | bytes 94371840 | tf_op jit(solution)/shard_map/correlate/pallas_call | solution.py:196
  (19 shorter events, 0.1 us)
Async XLA Ops:
  0.0 9.6 %copy-start = (s32[512]{0:T(512)S(1)}, s32[512]{0:T(512)}, u32[]{:S(2)}) copy-start(s32[512]{0:T(512)} %param.10) | copy-start | bytes 6148
  0.0 14.7 %copy-start.9 = (s32[4]{0:T(128)S(1)}, s32[4]{0:T(128)}, u32[]{:S(2)}) copy-start(s32[4]{0:T(128)} %param.11) | copy-start | bytes 52
  0.0 15.1 %copy-start.4 = (s32[512]{0:T(512)S(1)}, s32[512]{0:T(512)}, u32[]{:S(2)}) copy-start(s32[512]{0:T(512)} %param.12) | copy-start | bytes 6148
  3.5 39.7 %copy-start.5 = (f32[2048]{0:T(1024)S(1)}, f32[2048]{0:T(1024)}, u32[]{:S(2)}) copy-start(f32[2048]{0:T(1024)} %constant.38.clone) | copy-start | bytes 24580
  3.5 39.7 %copy-start.6 = (f32[2048]{0:T(1024)S(1)}, f32[2048]{0:T(1024)}, u32[]{:S(2)}) copy-start(f32[2048]{0:T(1024)} %constant.37.clone) | copy-start | bytes 24580
  3.5 39.7 %copy-start.7 = (f32[2048]{0:T(1024)S(1)}, f32[2048]{0:T(1024)}, u32[]{:S(2)}) copy-start(f32[2048]{0:T(1024)} %constant.36.clone) | copy-start | bytes 24580
  3.5 39.7 %copy-start.8 = (f32[2048]{0:T(1024)S(1)}, f32[2048]{0:T(1024)}, u32[]{:S(2)}) copy-start(f32[2048]{0:T(1024)} %constant.12.clone) | copy-start | bytes 24580
  4.7 37.2 %collective-permute-start = (bf16[128,3,2048]{2,0,1:T(8,128)(2,1)S(1)}, bf16[128,3,2048]{2,0,1:T(8,128)(2,1)S(1)}, u32[]{:S(2)}, u32[]{:S(2)}) collective-permute-start(bf16[128,3,2048]{2,0,1:T(8,128)(2,1)S(1)} %copy.21), channel_id=1, source_target_pairs={{0,1},{1,2},{2,3},{4,5},{5,6},{6,7},{8,9},{9,10},{10,11},{12,13},{... | collective-permute-start | bytes 4718600 | tf_op jit(solution)/shard_map/ppermute | solution.py:22
  43.2 18.4 %copy-start.10 = (bf16[2,512,2048,1]{2,1,0,3:T(8,128)(2,1)S(1)}, bf16[2,512,2048,1]{2,1,0,3:T(8,128)(2,1)}, u32[]{:S(2)}) copy-start(bf16[2,512,2048,1]{2,1,0,3:T(8,128)(2,1)} %constant.40) | copy-start | bytes 12582916
  100.9 2.8 copy-start.3
  305.1 10.4 %copy-start.2 = (bf16[5,192,4,32,128]{4,3,2,1,0:T(8,128)(2,1)}, bf16[5,192,4,32,128]{4,3,2,1,0:T(8,128)(2,1)S(1)}, u32[]{:S(2)}) copy-start(bf16[5,192,4,32,128]{4,3,2,1,0:T(8,128)(2,1)S(1)} %exchange.1) | copy-start | bytes 94371840
  315.5 40.9 %copy-start.1 = (s32[512]{0:T(512)S(1)}, s32[512]{0:T(512)}, u32[]{:S(2)}) copy-start(s32[512]{0:T(512)} %param.10) | copy-start | bytes 6148
where the time goes:
time: 358 us; the launch traced here: 356 us
  Pallas kernels  242 us (68%)
  local copies, waits for them, and re-layouts  44.8 us (13%)
  matrix products  24 us (7%)
  waiting for transfers between devices  21.6 us (6%)
  other arithmetic  20.2 us (6%)
    pallas_call x1, Pallas kernels, exchange(): pl.pallas_call(functools.partial(exchange_kernel, cycle, owners, chunks,...  201 us
    pallas_call x1, Pallas kernels, correlate(): pl.pallas_call(functools.partial(correlate_kernel, owners), grid=(capacit...  40.9 us
    dot_general x1, matrix products, body(): jnp.einsum('pcs,ifs->cpfi', transform_table(), filtered, preferred_elemen...  24 us
    ppermute x1, waiting for transfers between devices, shifted(): lax.ppermute(value, axis, [(source, source + steps) for source in range(f...  21.6 us
    convert_element_type x1, other arithmetic, body(): filtered = filtered.astype(jnp.bfloat16)  18.4 us
    unnamed x23, local copies, waits for them, and re-layouts  14.3 us
    convert_element_type x1, local copies, waits for them, and re-layouts, body(): spectra = (spectra * normalizer).astype(jnp.bfloat16)  8.01 us
    gather x1, local copies, waits for them, and re-layouts, body(): jnp.take(spectra, channel, axis=0, mode='clip')  7.24 us
  transfers between devices with their start and end apart: 1, of which 1 were waited for; matrix products, arithmetic and copies ran while one was open for 3% of the time, Pallas kernels for 0%

commit v1 on v0

--- a/solution.py
+++ b/solution.py
@@ -34,8 +34,8 @@
 def transform_table():
     sample = np.arange(NSAMP, dtype=np.int64)
     channel_id = CH0 + np.arange(NCH, dtype=np.int64)
-    angles = 2 * np.pi / NSAMP * (sample[None, :] * channel_id[:, None] % NSAMP)
-    return np.stack([np.cos(angles), -np.sin(angles)], axis=0).astype(ml_dtypes.bfloat16)
+    angles = 2 * np.pi / NSAMP * (sample[:, None] * channel_id[None, :] % NSAMP)
+    return np.stack([np.cos(angles), -np.sin(angles)], axis=2).astype(ml_dtypes.bfloat16)
 
 
 def slot_tables(channel_order, owner_count, channel_good, capacity):
@@ -163,7 +163,7 @@
             pltpu.SemaphoreType.DMA((chunks, offsets)),
         ],
         compiler_params=pltpu.CompilerParams(
-            collective_id=0, has_side_effects=True, vmem_limit_bytes=16 * 1024 * 1024
+            collective_id=0, has_side_effects=True, vmem_limit_bytes=60 * 1024 * 1024
         ),
         cost_estimate=pl.CostEstimate(flops=0, bytes_accessed=moved, transcendentals=0),
         name="exchange",
@@ -184,11 +184,11 @@
             swapped.append(-own[low : low + half])
         turned = jnp.concatenate(swapped, axis=0)
         left = jnp.concatenate([own.T, turned.T], axis=0)
-        for o in range(offsets):
-            summed = jnp.dot(left, spectra_ref[o, m], preferred_element_type=jnp.float32) * scale
-            summed = summed.astype(jnp.bfloat16)
-            out_ref[0, m, :, o * width : (o + 1) * width] = summed[:width]
-            out_ref[1, m, :, o * width : (o + 1) * width] = summed[width:]
+        right = jnp.concatenate([spectra_ref[o, m] for o in range(offsets)], axis=1)
+        summed = jnp.dot(left, right, preferred_element_type=jnp.float32) * scale
+        summed = summed.astype(jnp.bfloat16)
+        out_ref[0, m] = summed[:width]
+        out_ref[1, m] = summed[width:]
 
 
 def correlate(spectra, factor, owners, slots):
@@ -227,14 +227,15 @@
         filtered = filtered + window[k] * padded[:, k : k + frame_count].astype(jnp.float32)
     filtered = filtered.astype(jnp.bfloat16)
     spectra = jnp.einsum(
-        "pcs,ifs->cpfi", transform_table(), filtered, preferred_element_type=jnp.float32
+        "ifs,scp->fcpi", filtered, transform_table(), preferred_element_type=jnp.float32
     )
-    spectra = (spectra * normalizer).astype(jnp.bfloat16)
+    spectra = lax.optimization_barrier((spectra * normalizer).astype(jnp.bfloat16))
+    spectra = spectra.transpose(1, 2, 0, 3)
     channel, slot_live = slot_tables(channel_order, owner_count, channel_good, capacity)
     outgoing = jnp.take(spectra, channel, axis=0, mode="clip").reshape(
         owners, capacity, 2 * frame_count, block_width
     )
-    chunks = max(1, capacity // 16)
+    chunks = max(1, capacity // 12)
     arrived = exchange(outgoing, cycle_size, owners, offset_count, chunks)
     arrived = arrived.reshape(offset_count, capacity, owners * 2 * frame_count, block_width)
     factor = (

time: 358 us -> 328 us (0.916)
  matrix products: 24 us -> 10.9 us
  local copies, waits for them, and re-layouts: 44.8 us -> 31.7 us
    unnamed x23 -> x19, local copies, waits for them, and re-layouts: 14.3 us -> 1.19 us
    dot_general x1, matrix products: 24 us -> 10.9 us  [body(): jnp.einsum('ifs,scp->fcpi', filtered, transform_table(), preferred_elemen...]
    convert_element_type x1 -> x0, local copies, waits for them, and re-layouts: 8.01 us -> none  [body(): spectra = (spectra * normalizer).astype(jnp.bfloat16)]
    transpose x0 -> x1, local copies, waits for them, and re-layouts: none -> 8 us  [body(): spectra = spectra.transpose(1, 2, 0, 3)]
    pallas_call x1, Pallas kernels: 201 us -> 198 us  [exchange(): pl.pallas_call(functools.partial(exchange_kernel, cycle, owners, chunks,...]
  transfers between devices with their start and end apart: 1 -> 1, of which waited for: 1 -> 1; matrix products, arithmetic and copies ran while one was open for 3% -> 4% of each run, Pallas kernels for 0% -> 0%
where the time goes in v1:
time: 328 us; the launch traced here: 326 us
  Pallas kernels  239 us (73%)
  local copies, waits for them, and re-layouts  31.7 us (10%)
  waiting for transfers between devices  21.5 us (7%)
  other arithmetic  20.2 us (6%)
  matrix products  10.9 us (3%)
  starting transfers between devices  3.39 us (1%)
    pallas_call x1, Pallas kernels, exchange(): pl.pallas_call(functools.partial(exchange_kernel, cycle, owners, chunks,...  198 us
    pallas_call x1, Pallas kernels, correlate(): pl.pallas_call(functools.partial(correlate_kernel, owners), grid=(capacit...  40.9 us
    ppermute x1, waiting for transfers between devices, shifted(): lax.ppermute(value, axis, [(source, source + steps) for source in range(f...  21.5 us
    convert_element_type x1, other arithmetic, body(): filtered = filtered.astype(jnp.bfloat16)  18.4 us
    dot_general x1, matrix products, body(): jnp.einsum('ifs,scp->fcpi', filtered, transform_table(), preferred_elemen...  10.9 us
    transpose x1, local copies, waits for them, and re-layouts, body(): spectra = spectra.transpose(1, 2, 0, 3)  8 us
    gather x1, local copies, waits for them, and re-layouts, body(): jnp.take(spectra, channel, axis=0, mode='clip')  7.24 us
  transfers between devices with their start and end apart: 1, of which 1 were waited for; matrix products, arithmetic and copies ran while one was open for 4% of the time, Pallas kernels for 0%

profile of v1, /device:TPU:9, one launch (start us, length us, event | category | flops | bytes accessed | tf_op | source)
XLA Modules:
  0.0 326.3 jit_solution(7081580499084058438)
XLA Ops:
  0.0 3.5 %slice.12 = bf16[128,3,2048]{2,1,0:T(4,128)(2,1)S(1)} slice(bf16[128,16,2048]{2,1,0:T(8,128)(2,1)} %param.9), slice={[0:128], [13:16], [0:2048]} | slice | bytes 3145728 | tf_op jit(solution)/shard_map/slice | solution.py:223
  3.5 0.0 copy-start.3
  3.5 0.0 copy-start.4
  3.5 0.0 copy-start.5
  3.5 0.0 copy-start.6
  3.5 1.1 copy.21
  4.7 3.4 %collective-permute-start = (bf16[128,3,2048]{2,0,1:T(8,128)(2,1)S(1)}, bf16[128,3,2048]{2,0,1:T(8,128)(2,1)S(1)}, u32[]{:S(2)}, u32[]{:S(2)}) collective-permute-start(bf16[128,3,2048]{2,0,1:T(8,128)(2,1)S(1)} %copy.21), channel_id=1, source_target_pairs={{0,1},{1,2},{2,3},{4,5},{5,6},{6,7},{8,9},{9,10},{10,11},{12,13},{... | collective-permute-start | bytes 4718600 | tf_op jit(solution)/shard_map/ppermute | solution.py:22
  8.1 0.8 reduce-window.9
  8.9 0.7 bitcast_subtract_fusion
  9.6 0.1 compare_select_fusion.1
  9.7 0.1 reshape.150
  9.7 0.0 copy-done
  9.7 5.0 %gather_fusion = s32[768]{0:T(1024)S(1)} fusion(s32[512]{0:T(512)S(1)} %copy-done, s32[1024]{0:T(1024)S(1)} %pad_clamp_fusion.2), kind=kCustom, calls=%fused_computation | custom fusion | bytes 9216 | tf_op jit(solution)/shard_map/gather | solution.py:46
  14.8 0.1 reshape.149
  14.8 0.1 broadcast_select_fusion.1
  14.9 0.1 select_n.48
  15.0 0.1 reshape.166
  15.1 0.1 iota_compare_fusion
  15.1 0.1 lt.68
  15.3 5.0 %gather_fusion.1 = s32[768]{0:T(1024)S(1)} fusion(s32[512]{0:T(512)S(1)} %copy-done.2, s32[1024]{0:T(1024)S(1)} %pad_clamp_fusion.1), kind=kCustom, calls=%fused_computation.1 | custom fusion | bytes 9216 | tf_op jit(solution)/shard_map/gather | solution.py:47
  20.3 0.1 convert_multiply_fusion.factor_ref
  20.4 21.5 %collective-permute-done = bf16[128,3,2048]{2,0,1:T(8,128)(2,1)S(1)} collective-permute-done((bf16[128,3,2048]{2,0,1:T(8,128)(2,1)S(1)}, bf16[128,3,2048]{2,0,1:T(8,128)(2,1)S(1)}, u32[]{:S(2)}, u32[]{:S(2)}) %collective-permute-start) | collective-permute-done | bytes 1572896 | tf_op jit(solution)/shard_map/ppermute | solution.py:22
  41.9 1.4 copy.15
  43.2 0.0 copy-done.3
  43.2 0.0 copy-start.8
  43.3 18.4 %fusion.4 = bf16[128,16,2048,1]{2,1,0,3:T(8,128)(2,1)S(1)} fusion(bf16[128,16,2048]{2,1,0:T(8,128)(2,1)} %param.9, f32[2048]{0:T(1024)S(1)} %copy-done.3, bf16[128,3,2048]{2,1,0:T(4,128)(2,1)S(1)} %copy.15, f32[2048]{0:T(1024)S(1)} %copy-done.4, f32[2048]{0:T(1024)S(1)} %copy-done.5, f32[2048]{0:T(1024)S(1)} %copy-done.6), kind=kLoop, calls=%fused_computation.14 | loop fusion | flops 88080384 | bytes 18382848 | tf_op jit(solution)/shard_map/convert_element_type | solution.py:228
  61.6 10.9 %fusion.5 = bf16[16,512,2,128]{1,3,2,0:T(8,128)(2,1)} fusion(bf16[2048,512,2,1]{1,0,2,3:T(8,128)(2,1)S(1)} %copy-done.8, bf16[128,16,2048,1]{2,1,0,3:T(8,128)(2,1)S(1)} %fusion.4), kind=kOutput, calls=%fused_computation.15 | convolution fusion | flops 8594128896 | bytes 16777216 | tf_op jit(solution)/shard_map/ifs,scp->fcpi/dot_general | solution.py:229
  72.5 8.0 %copy.17 = bf16[512,2,16,128]{3,2,1,0:T(8,128)(2,1)} copy(bf16[512,2,16,128]{0,3,1,2:T(8,128)(2,1)} %bitcast.16) | data formatting | bytes 8388608 | tf_op jit(solution)/shard_map/transpose | solution.py:233
  80.5 7.2 %gather_fusion.2 = bf16[768,2,16,128]{3,2,1,0:T(8,128)(2,1)} fusion(bf16[512,2,16,128]{3,2,1,0:T(8,128)(2,1)} %copy.17, s32[1024]{0:T(1024)S(1)} %pad_clamp_fusion), kind=kCustom, calls=%fused_computation.2 | custom fusion | bytes 12585984 | tf_op jit(solution)/shard_map/jit(_take)/gather | solution.py:235
  87.8 197.6 %exchange.1 = bf16[5,192,4,32,128]{4,3,2,1,0:T(8,128)(2,1)} custom-call(bf16[4,192,32,128]{3,2,1,0:T(8,128)(2,1)} %bitcast.15), custom_call_target="tpu_custom_call" | custom-call | bytes 37748736 | tf_op jit(solution)/shard_map/exchange/pallas_call | solution.py:153
  285.4 0.0 copy-start.1
  285.4 40.9 %correlate.1 = bf16[2,192,128,640]{3,2,1,0:T(8,128)(2,1)} custom-call(f32[192]{0:T(256)S(1)} %convert_multiply_fusion.factor_ref, bf16[5,192,128,128]{3,2,1,0:T(8,128)(2,1)} %bitcast.14), custom_call_target="tpu_custom_call" | custom-call | flops 8053063680 | bytes 94371840 | tf_op jit(solution)/shard_map/correlate/pallas_call | solution.py:196
  (15 shorter events, 0.1 us)
Async XLA Ops:
  0.0 9.7 %copy-start = (s32[512]{0:T(512)S(1)}, s32[512]{0:T(512)}, u32[]{:S(2)}) copy-start(s32[512]{0:T(512)} %param.10) | copy-start | bytes 6148
  0.0 14.8 %copy-start.7 = (s32[4]{0:T(128)S(1)}, s32[4]{0:T(128)}, u32[]{:S(2)}) copy-start(s32[4]{0:T(128)} %param.11) | copy-start | bytes 52
  0.0 15.3 %copy-start.2 = (s32[512]{0:T(512)S(1)}, s32[512]{0:T(512)}, u32[]{:S(2)}) copy-start(s32[512]{0:T(512)} %param.12) | copy-start | bytes 6148
  3.5 39.7 %copy-start.3 = (f32[2048]{0:T(1024)S(1)}, f32[2048]{0:T(1024)}, u32[]{:S(2)}) copy-start(f32[2048]{0:T(1024)} %constant.38.clone) | copy-start | bytes 24580
  3.5 39.7 %copy-start.4 = (f32[2048]{0:T(1024)S(1)}, f32[2048]{0:T(1024)}, u32[]{:S(2)}) copy-start(f32[2048]{0:T(1024)} %constant.37.clone) | copy-start | bytes 24580
  3.5 39.7 %copy-start.5 = (f32[2048]{0:T(1024)S(1)}, f32[2048]{0:T(1024)}, u32[]{:S(2)}) copy-start(f32[2048]{0:T(1024)} %constant.36.clone) | copy-start | bytes 24580
  3.5 39.7 %copy-start.6 = (f32[2048]{0:T(1024)S(1)}, f32[2048]{0:T(1024)}, u32[]{:S(2)}) copy-start(f32[2048]{0:T(1024)} %constant.12.clone) | copy-start | bytes 24580
  4.7 37.2 %collective-permute-start = (bf16[128,3,2048]{2,0,1:T(8,128)(2,1)S(1)}, bf16[128,3,2048]{2,0,1:T(8,128)(2,1)S(1)}, u32[]{:S(2)}, u32[]{:S(2)}) collective-permute-start(bf16[128,3,2048]{2,0,1:T(8,128)(2,1)S(1)} %copy.21), channel_id=1, source_target_pairs={{0,1},{1,2},{2,3},{4,5},{5,6},{6,7},{8,9},{9,10},{10,11},{12,13},{... | collective-permute-start | bytes 4718600 | tf_op jit(solution)/shard_map/ppermute | solution.py:22
  43.2 18.4 %copy-start.8 = (bf16[2048,512,2,1]{1,0,2,3:T(8,128)(2,1)S(1)}, bf16[2048,512,2,1]{1,0,2,3:T(8,128)(2,1)}, u32[]{:S(2)}) copy-start(bf16[2048,512,2,1]{1,0,2,3:T(8,128)(2,1)} %constant.40) | copy-start | bytes 12582916
  285.4 40.9 %copy-start.1 = (s32[512]{0:T(512)S(1)}, s32[512]{0:T(512)}, u32[]{:S(2)}) copy-start(s32[512]{0:T(512)} %param.10) | copy-start | bytes 6148
